TPU v7x, 256 devices: a whole 4x4x8 slice. The times are simulated.
256 devices in a mesh: row: 16 (over y_lo, z), col: 16 (over x, y_hi, core).
Axes of the slice: x: 4, y: 4 (y_hi: 2, y_lo: 2; y = y_hi * 2 + y_lo), z: 8, core: 2. Of those that a mesh axis runs over, the one named last changes fastest.
Arguments:
- amplitudes: bfloat16 [6400, 200704], P('row', 'col'), may hold values from -6 to 6
- integrals: bfloat16 [1024, 200704], P('row', 'col'), may hold values from -0.01953125 to 0.01953125
- residual_in: float32 [1024, 6400], P('col', 'row'), may hold values from -6 to 6
Outputs:
- residual_out: float32 [1024, 6400], P('col', 'row')
All inputs are finite; a program needn't handle non-finite values.
Results may differ from a plain program's by a relative error of at most 0.0003.
Values may be sent and summed in bfloat16 or wider, within the bound.
A program may use at most 128 MiB of HBM per device.

v0:
```python
import jax
import jax.numpy as jnp
from jax import lax
from jax.experimental import pallas as pl
from jax.experimental.pallas import tpu as pltpu
from jax.sharding import PartitionSpec as P

MESH = pl.DeviceIdType.MESH
NT = (((1,), (1,)), ((), ()))
RING = 8
BLOCK = 64
OCC = 5
NOCC = 80
HALF_J = 40
SUB = 2
STEPS = 7
LANES = 2 * BLOCK
CUTS = (0, 22, 41, 49)


def differs(a, b):
    return a + b - 2 * a * b


def kernel(
    amp, integ, out, rows_a, ints, sums, from_core, from_x, late_in, from_all, from_last, to_y, from_y,
    total, to_mirror, from_mirror, to_late, from_late, direct_half, turned, upright,
    local_sem, iy_s, iy_r, ay_s, ay_r, al_s, al_r, up_s, up_r, dn_s, dn_r, c_s, c_r, x_s, x_r, lc_s, lc_r, all_s, all_r, last_s, last_r,
    y_s, y_r, m_s, m_r, lm_s, lm_r, d_s, d_r,
):
    row, col = lax.axis_index("row"), lax.axis_index("col")
    y, z = row // RING, row % RING
    hx, zx, yh, core = col // 8, (col // 4) % 2, (col // 2) % 2, col % 2
    half = integ.shape[1] // 2
    mine = pl.ds(pl.multiple_of(y * half, 128), half)
    theirs = pl.ds(pl.multiple_of((1 - y) * half, 128), half)
    cuts = [(128 * a, 128 * (b - a)) for a, b in zip(CUTS[:-1], CUTS[1:])]

    def dev(y_=y, z_=z, hx_=hx, zx_=zx, yh_=yh, core_=core):
        return (y_ * RING + z_, hx_ * 8 + zx_ * 4 + yh_ * 2 + core_)

    def group(distance):
        return (z + distance + RING) % RING

    def slot(d):
        return (d % 2) * 4 + d // 2

    def remote(src, dst, send, recv, device):
        return pltpu.make_async_remote_copy(
            src_ref=src, dst_ref=dst, send_sem=send, recv_sem=recv, device_id=device, device_id_type=MESH
        )

    barrier = pltpu.get_barrier_semaphore()

    def greet(device):
        pl.semaphore_signal(barrier, inc=1, device_id=device, device_id_type=MESH)

    near = [dev(z_=group(1)), dev(z_=group(-1)), dev(core_=1 - core)]
    for device in near:
        greet(device)

    def is_me(h, y_, z_):
        return jnp.logical_and(jnp.logical_and(h == hx, y_ == y), z_ == z)

    def greet_source(t, _):
        greet(((1 - y) * RING + z, 2 * t + core))

        @pl.when(2 * t + core != col)
        def _():
            greet((row, 2 * t + core))

        for y_ in range(2):

            @pl.when(jnp.logical_not(is_me(y, y_, t)))
            def _(y_=y_):
                greet(dev(hx_=y, y_=y_, z_=t))

        return 0

    lax.fori_loop(0, RING, greet_source, 0)
    pl.semaphore_wait(barrier, len(near) + 4 * RING - 1 - (1 - differs(hx, y)))

    upright[pl.ds(OCC * NOCC, 4 * LANES - OCC * NOCC), :] = jnp.zeros((4 * LANES - OCC * NOCC, LANES), jnp.float32)

    def cut_along_q(m):
        return m >= STEPS - 2

    def pieces(m):
        return range(len(cuts) if cut_along_q(m) else SUB)

    def block_at(distance, owner_y, m, u):
        if cut_along_q(m):
            start, size, columns = 0, BLOCK, pl.ds(*cuts[u])
        else:
            start, size, columns = u * (BLOCK // SUB), BLOCK // SUB, pl.ds(0, half)
        start = pl.multiple_of(owner_y * BLOCK + start, BLOCK // SUB)
        return ints.at[slot(distance % RING), pl.ds(start, size), columns]

    def sub(u):
        return pl.ds(u * (BLOCK // SUB), BLOCK // SUB)

    def up_block(m):
        return -(m // 2), y if m % 2 == 0 else 1 - y

    def down_block(m):
        return (0, 0, 1, 1, 2, 2, 3)[m], (y, 1 - y, y, 1 - y, 1 - y, y, 1 - y)[m]

    def up(m, u):
        distance, owner = up_block(m)
        src = integ.at[sub(u), mine] if m == 0 else block_at(distance, owner, m, u)
        return remote(src, block_at(distance - 1, owner, m, u), up_s.at[m, u], up_r.at[m, u], dev(z_=group(1)))

    def down(m, u):
        distance, owner = down_block(m)
        src = integ.at[sub(u), mine] if m == 0 else block_at(distance, owner, m, u)
        return remote(src, block_at(distance + 1, owner, m, u), dn_s.at[m, u], dn_r.at[m, u], dev(z_=group(-1)))

    def up_arrives(n, u):
        distance, owner = up_block(n)
        place = block_at(distance - 1, owner, n, u)
        remote(place, place, up_s.at[n, u], up_r.at[n, u], dev(z_=group(1))).wait_recv()

    def down_arrives(n, u):
        distance, owner = down_block(n)
        place = block_at(distance + 1, owner, n, u)
        remote(place, place, dn_s.at[n, u], dn_r.at[n, u], dev(z_=group(-1))).wait_recv()

    def swap_i(u):
        return remote(integ.at[sub(u), theirs], block_at(0, y, 0, u), iy_s.at[u], iy_r.at[u], dev(y_=1 - y))

    def swap_i_arrives(u):
        place = block_at(0, 1 - y, 0, u)
        remote(place, place, iy_s.at[u], iy_r.at[u], dev(y_=1 - y)).wait_recv()

    def swap_a(i):
        src, dst = amp.at[pl.ds(i * NOCC, NOCC), theirs], rows_a.at[pl.ds((OCC + i) * NOCC, NOCC)]
        return remote(src, dst, ay_s.at[i], ay_r.at[i], dev(y_=1 - y))

    def swap_cut(i, k):
        start, width = cuts[k]
        src = amp.at[pl.ds(i * NOCC, NOCC), pl.ds(pl.multiple_of((1 - y) * half + start, 128), width)]
        dst = rows_a.at[pl.ds((OCC + i) * NOCC, NOCC), pl.ds(start, width)]
        return remote(src, dst, al_s.at[i - OCC + 2, k], al_r.at[i - OCC + 2, k], dev(y_=1 - y))

    for u in range(SUB):
        swap_i(u).start()
        up(0, u).start()
        down(0, u).start()
    own_rows = pl.ds(pl.multiple_of(y * BLOCK, BLOCK), BLOCK)
    load_i = pltpu.make_async_copy(integ.at[:, mine], ints.at[slot(0), own_rows], local_sem.at[0])
    load_a = pltpu.make_async_copy(amp.at[:, mine], rows_a.at[pl.ds(0, OCC * NOCC)], local_sem.at[1])
    load_i.start()
    load_a.start()
    for u in range(SUB):
        swap_i_arrives(u)
        up(1, u).start()
        down(1, u).start()
        if u == 0:
            swap_a(0).start()
    swap_a(1).start()
    load_i.wait()
    load_a.wait()

    def product(first, count, at, blocks, k=None):
        columns, width = (pl.ds(0, half), half) if k is None else (pl.ds(*cuts[k]), cuts[k][1])
        value = lax.dot_general(
            rows_a[pl.ds(first * NOCC, count * NOCC), columns],
            ints[pl.ds(at, blocks), :, columns].reshape(blocks * LANES, width),
            NT,
            preferred_element_type=jnp.float32,
        )
        for q in range(blocks):
            part = value[:, q * LANES : (q + 1) * LANES].reshape(count, NOCC, LANES)
            if k is None or k == 0:
                sums[at + q, pl.ds(first, count)] = part
            else:
                sums[at + q, pl.ds(first, count)] += part

    def five_blocks(first, k=None):
        product(first, 1, slot(0), 2, k)
        product(first, 1, slot(6), 2, k)
        product(first, 1, slot(7), 1, k)

    def part_of(role):
        return (pl.ds(0, OCC), pl.ds(OCC, OCC - 2), pl.ds(2 * OCC - 2, 1), pl.ds(0, 2 * OCC - 1))[role]

    def is_kept(d):
        return group(d) % 2 == core

    def to_core(d, role):
        at = part_of(role)
        return remote(
            sums.at[slot(d), at], from_core.at[d // 2, at], c_s.at[d // 2, role % 3], c_r.at[d // 2, role % 3], dev(core_=1 - core)
        )

    def to_x(d, role, h, act):
        at, g = part_of(role), group(d)
        z2, z1 = g // 4, (g // 2) % 2
        delta = 2 * differs(h, hx) + differs(z2, zx)

        @pl.when(delta > 0)
        def _():
            act(
                remote(
                    sums.at[slot(d), at, pl.ds(h * HALF_J, HALF_J)], from_x.at[delta - 1, z1, at],
                    x_s.at[d // 2, role % 3, h], x_r.at[delta - 1, z1], dev(hx_=h, zx_=z2),
                )
            )

    def reduce_core(d, role):
        @pl.when(jnp.logical_not(is_kept(d)))
        def _():
            to_core(d, role).start()

    def reduce_x(d, role):
        @pl.when(is_kept(d))
        def _():
            to_core(d, role).wait_recv()
            at = part_of(role)
            sums[slot(d), at] += from_core[d // 2, at]
            for h in range(2):
                to_x(d, role, h, lambda copy: copy.start())

    def over_five(act):
        lax.fori_loop(0, 5, lambda t, _: (act(t + 3 * (t // 3)), 0)[1], 0)

    last = group(4)
    j_mine = pl.ds(pl.multiple_of(hx * HALF_J, 8), HALF_J)
    j_theirs = pl.ds(pl.multiple_of((1 - hx) * HALF_J, 8), HALF_J)
    most = pl.ds(0, OCC - 1)

    def unit(z1):
        return zx * 4 + z1 * 2 + core

    def kept_of(far):
        return most if far else pl.ds(0, OCC)

    def x_arrives(z1):
        for delta in range(3):
            place = from_x.at[delta, z1]
            remote(place, place, x_s.at[0, 0, 0], x_r.at[delta, z1], dev(hx_=1 - hx)).wait_recv()

    def x_sum(z1, far):
        at = pl.ds(OCC, OCC - 1) if far else pl.ds(0, OCC)
        value = sums[slot((unit(z1) - z + RING) % RING), at, j_mine, :]
        for delta in range(3):
            value = value + from_x[delta, z1, at]
        return value

    def y_copy(e):
        at = kept_of(e & 1)
        target = dev(yh_=1 - yh if e & 2 else yh, y_=1 - y if e & 1 else y)
        return remote(to_y.at[e - 1, at], from_y.at[e - 1, at], y_s.at[e - 1], y_r.at[e - 1], target)

    def y_send(e):
        to_y[e - 1, kept_of(e & 1)] = x_sum(1 - yh if e & 2 else yh, e & 1)
        y_copy(e).start()

    def y_stage():
        @pl.when(unit(1 - yh) != last)
        def _():
            x_arrives(1 - yh)
            y_send(2)
            y_send(3)

        @pl.when(unit(yh) != last)
        def _():
            x_arrives(yh)
            y_send(1)
            total[...] = x_sum(yh, 0)

    def y_sent():
        @pl.when(unit(1 - yh) != last)
        def _():
            y_copy(2).wait_send()
            y_copy(3).wait_send()

        @pl.when(unit(yh) != last)
        def _():
            y_copy(1).wait_send()

    def to_last(h, far):
        at = pl.ds(OCC, OCC - 1) if far else pl.ds(0, OCC)
        sender = y * RING + col // 2
        z2, z1 = last // 4, (last // 2) % 2
        target = dev(y_=1 - y if far else y, hx_=h, zx_=z2, yh_=z1)
        return remote(
            sums.at[slot(4), at, pl.ds(h * HALF_J, HALF_J)], from_last.at[sender, kept_of(far)],
            last_s.at[h, far], last_r.at[sender], target,
        )

    def each_last(act):
        for far in (1, 0):
            for h in range(2):
                if far:
                    act(to_last(h, far))
                else:

                    @pl.when(jnp.logical_not(jnp.logical_and(unit(yh) == last, h == hx)))
                    def _(h=h, far=far):
                        act(to_last(h, far))

    def reduce_last():
        @pl.when(is_kept(4))
        def _():
            to_core(4, 3).wait_recv()
            at = part_of(3)
            sums[slot(4), at] += from_core[2, at]
            each_last(lambda copy: copy.start())

    def last_sums():
        value = sums[slot(4), pl.ds(0, OCC), j_mine, :]
        total[...] = value

        def add(t, _):
            @pl.when(2 * t + core != col)
            def _():
                place = from_last.at[y * RING + t]
                remote(place, place, last_s.at[0, 0], last_r.at[y * RING + t], dev(hx_=1 - hx)).wait_recv()
                total[...] += from_last[y * RING + t]

            there = (1 - y) * RING + t
            place = from_last.at[there, most]
            remote(place, place, last_s.at[0, 0], last_r.at[there], dev(hx_=1 - hx)).wait_recv()
            total[most] += from_last[there, most]
            return 0

        lax.fori_loop(0, RING, add, 0)

    mirror = dev(hx_=1 - hx)

    def direct(k):
        at = pl.ds(OCC - 1, 1) if k else most
        return remote(total.at[at], direct_half.at[at], d_s.at[k], d_r.at[k], mirror)

    def mirror_copy(k, t, h):
        src, dst, send, recv = ((to_mirror, from_mirror, m_s, m_r), (to_late, from_late, lm_s, lm_r))[k]
        return remote(src.at[t], dst.at[row], send.at[t, h], recv.at[row], dev(hx_=h, y_=hx, z_=t))

    def each_mirror(act):
        def body(t, _):
            for h in range(2):

                @pl.when(jnp.logical_not(is_me(h, hx, t)))
                def _():
                    act(t, h)

            return 0

        lax.fori_loop(0, RING, body, 0)

    def mirror_arrives(k):
        dst, send, recv = ((from_mirror, m_s, m_r), (from_late, lm_s, lm_r))[k]

        def body(r, _):
            @pl.when(jnp.logical_not(is_me(y, r // RING, r % RING)))
            def _():
                place = dst.at[r]
                remote(place, place, send.at[0, 0], recv.at[r], mirror).wait_recv()

            return 0

        lax.fori_loop(0, 2 * RING, body, 0)

    def spread():
        direct(0).start()
        for t in range(RING):
            for b in range(OCC):
                to_mirror[t, pl.ds(b * 4, 4), :] = total[most, t * OCC + b, :]
        each_mirror(lambda t, h: mirror_copy(0, t, h).start())

        @pl.when(hx == y)
        def _():
            from_mirror[row] = to_mirror[z]

    kept = (z + core) % 2
    late_core = remote(
        sums.at[pl.ds(4 * (1 - kept), 4), 2 * OCC - 1], late_in, lc_s, lc_r, dev(core_=1 - core)
    )

    def to_owner(q, h):
        d = 2 * q + kept
        src = sums.at[slot(d), 2 * OCC - 1, pl.ds(h * HALF_J, HALF_J)]
        owner = h * RING + group(d)
        return remote(src, from_all.at[col // 2], all_s.at[q, h], all_r.at[col // 2], ((1 - y) * RING + z, owner))

    def each_owner(act):
        def body(q, _):
            for h in range(2):
                act(to_owner(q, h))
            return 0

        lax.fori_loop(0, RING // 2, body, 0)

    product(0, OCC, slot(0), 1)
    reduce_core(0, 0)
    for n in range(STEPS - 2):
        if n == 4:
            for k in pieces(5):
                down(5, k).start()
        for u in pieces(n):
            up_arrives(n, u)
            if n + 2 < STEPS - 2:
                up(n + 2, u).start()
            down_arrives(n, u)
            if n in (0, 1):
                down(n + 2, u).start()
            elif n == 3:
                down(4, u).start()
        if n == 3:
            for k in pieces(5):
                up(5, k).start()
        elif n == 4:
            for k in pieces(6):
                up(6, k).start()
                down(6, k).start()
        if n == 1:
            swap_a(2).start()
        elif n in (2, 3):
            for k in range(len(cuts)):
                swap_cut(n + 1, k).start()
        if n == 0:
            reduce_x(0, 0)
        elif n in (1, 3):
            d = (n + 1) // 2
            for distance in (d, RING - d):
                product(0, OCC + d - 1, slot(distance), 1)
                reduce_core(distance, 0)
            for distance in (d, RING - d):
                reduce_x(distance, 0)
        if n == 2:
            swap_a(0).wait_recv()
            for distance in (0, 1, 7):
                product(OCC, 1, slot(distance), 1)
        elif n == 3:
            swap_a(1).wait_recv()
            five_blocks(OCC + 1)
        elif n == 4:
            swap_a(2).wait_recv()
            five_blocks(OCC + 2)
            over_five(lambda d: reduce_core(d, 1))
            over_five(lambda d: reduce_x(d, 1))

    def ring_sent(steps):
        for m in steps:
            for u in pieces(m):
                up(m, u).wait_send()
                down(m, u).wait_send()

    def sums_sent(d, role):
        @pl.when(jnp.logical_not(is_kept(d)))
        def _():
            to_core(d, role).wait_send()

        @pl.when(is_kept(d))
        def _():
            if isinstance(d, int) and d == 4:
                each_last(lambda copy: copy.wait_send())
            else:
                for h in range(2):
                    to_x(d, role, h, lambda copy: copy.wait_send())

    for u in range(SUB):
        swap_i(u).wait_send()
    ring_sent(range(4))
    for i in range(2):
        swap_a(i).wait_send()

    for k in range(len(cuts)):
        up_arrives(5, k)
        down_arrives(5, k)
        swap_cut(3, k).wait_recv()
        product(0, 2 * OCC - 1, slot(3), 2, k)
        five_blocks(2 * OCC - 2, k)
    for d in (3, 5):
        reduce_core(d, 3)
    over_five(lambda d: reduce_core(d, 2))
    for d in (3, 5):
        reduce_x(d, 3)
    over_five(lambda d: reduce_x(d, 2))

    ring_sent((4,))
    swap_a(2).wait_send()
    for role in range(2):
        over_five(lambda d, role=role: sums_sent(d, role))

    final = len(cuts) - 1
    for k in range(len(cuts)):
        up_arrives(6, k)
        down_arrives(6, k)
        product(0, 2 * OCC - 1, slot(4), 1, k)
        if k == 0:
            y_stage()
        if k == final:
            reduce_core(4, 3)
        for late in {0: (0,), final: range(1, final)}.get(k, ()):
            swap_cut(4, late).wait_recv()
            product(2 * OCC - 1, 1, 0, 4, late)
            product(2 * OCC - 1, 1, 4, 4, late)
    reduce_last()
    swap_cut(4, final).wait_recv()
    product(2 * OCC - 1, 1, 4 * (1 - kept), 4, final)
    late_core.start()
    product(2 * OCC - 1, 1, 4 * kept, 4, final)
    late_core.wait_recv()
    sums[pl.ds(4 * kept, 4), 2 * OCC - 1] += late_in[...]
    each_owner(lambda copy: copy.start())

    @pl.when(unit(yh) != last)
    def _():
        for e in (2, 3, 1):
            y_copy(e).wait_recv()
        total[...] += from_y[1]
        total[most] += from_y[0, most] + from_y[2, most]
        spread()

    @pl.when(unit(yh) == last)
    def _():
        last_sums()
        spread()

    def late_arrives(r, _):
        place = from_all.at[r]
        remote(place, place, all_s.at[0, 0], all_r.at[r], mirror).wait_recv()
        return 0

    lax.fori_loop(0, RING, late_arrives, 0)
    value = total[OCC - 1]
    for r in range(RING):
        value = value + from_all[r]
    total[OCC - 1] = value
    for t in range(RING):
        to_late[t, pl.ds(0, OCC), :] = total[OCC - 1, pl.ds(t * OCC, OCC), :]
    each_mirror(lambda t, h: mirror_copy(1, t, h).start())
    direct(1).start()

    @pl.when(hx == y)
    def _():
        from_late[row] = to_late[z]

    ring_sent((5, 6))
    for k in range(len(cuts)):
        swap_cut(3, k).wait_send()
        swap_cut(4, k).wait_send()
    over_five(lambda d: sums_sent(d, 2))
    for d in (3, 4, 5):
        sums_sent(d, 3)

    late_core.wait_send()
    each_owner(lambda copy: copy.wait_send())
    y_sent()
    mirror_arrives(0)
    for r in range(2 * RING):
        for b in range(OCC):
            turned[b, pl.ds(r * OCC, OCC - 1), :] = from_mirror[r, pl.ds(b * 4, 4), :]
    direct(0).wait_recv()

    direct(0).wait_send()
    each_mirror(lambda t, h: mirror_copy(0, t, h).wait_send())
    direct(1).wait_send()
    each_mirror(lambda t, h: mirror_copy(1, t, h).wait_send())
    mirror_arrives(1)
    for r in range(2 * RING):
        turned[:, r * OCC + OCC - 1, :] = from_late[r, pl.ds(0, OCC), :]
    direct(1).wait_recv()

    def finish(straight, swapped):
        straight, swapped = (v.reshape(OCC * HALF_J, LANES) for v in (straight, swapped))
        here = jnp.where(hx == 0, straight, swapped)
        there = jnp.where(hx == 0, swapped, straight)
        value = here + pltpu.roll(there, BLOCK, 1)
        return [value[i * HALF_J : (i + 1) * HALF_J] for i in range(OCC)]

    for h, straight in ((hx, total), (1 - hx, direct_half)):
        at = pl.ds(pl.multiple_of(h * HALF_J, 8), HALF_J)
        for i, value in enumerate(finish(straight[...], turned[:, at, :])):
            upright[pl.ds(pl.multiple_of(i * NOCC + h * HALF_J, 8), HALF_J), :] = value
    out[...] = upright[...].T[:BLOCK, : OCC * NOCC]


def on_device(amplitudes, integrals, residual_in):
    pairs, depth = amplitudes.shape
    half = depth // 2
    bf16, f32 = jnp.bfloat16, jnp.float32
    dma = pltpu.SemaphoreType.DMA
    cuts = len(CUTS) - 1
    ladder = pl.pallas_call(
        kernel,
        out_shape=jax.ShapeDtypeStruct((BLOCK, pairs), f32),
        in_specs=[pl.BlockSpec(memory_space=pltpu.HBM)] * 2,
        out_specs=pl.BlockSpec(memory_space=pltpu.VMEM),
        scratch_shapes=[
            pltpu.VMEM((2 * pairs, half), bf16),
            pltpu.VMEM((RING, LANES, half), bf16),
            pltpu.VMEM((RING, 2 * OCC, NOCC, LANES), f32),
            pltpu.VMEM((RING // 2, 2 * OCC - 1, NOCC, LANES), f32),
            pltpu.VMEM((3, 2, 2 * OCC - 1, HALF_J, LANES), f32),
            pltpu.VMEM((RING // 2, NOCC, LANES), f32),
            pltpu.VMEM((RING, HALF_J, LANES), f32),
            pltpu.VMEM((2 * RING, OCC, HALF_J, LANES), f32),
            pltpu.VMEM((3, OCC, HALF_J, LANES), f32),
            pltpu.VMEM((3, OCC, HALF_J, LANES), f32),
            pltpu.VMEM((OCC, HALF_J, LANES), f32),
            pltpu.VMEM((RING, 24, LANES), f32),
            pltpu.VMEM((2 * RING, 24, LANES), f32),
            pltpu.VMEM((RING, 8, LANES), f32),
            pltpu.VMEM((2 * RING, 8, LANES), f32),
            pltpu.VMEM((OCC, HALF_J, LANES), f32),
            pltpu.VMEM((OCC, NOCC, LANES), f32),
            pltpu.VMEM((4 * LANES, LANES), f32),
            dma((2,)),
            dma((SUB,)),
            dma((SUB,)),
            dma((OCC - 2,)),
            dma((OCC - 2,)),
            dma((2, cuts)),
            dma((2, cuts)),
            dma((STEPS, cuts)),
            dma((STEPS, cuts)),
            dma((STEPS, cuts)),
            dma((STEPS, cuts)),
            dma((RING // 2, 3)),
            dma((RING // 2, 3)),
            dma((RING // 2, 3, 2)),
            dma((3, 2)),
            dma,
            dma,
            dma((RING // 2, 2)),
            dma((RING,)),
            dma((2, 2)),
            dma((2 * RING,)),
            dma((3,)),
            dma((3,)),
            dma((RING, 2)),
            dma((2 * RING,)),
            dma((RING, 2)),
            dma((2 * RING,)),
            dma((2,)),
            dma((2,)),
        ],
        compiler_params=pltpu.CompilerParams(
            collective_id=0, has_side_effects=True, vmem_limit_bytes=53 * 1024 * 1024
        ),
        cost_estimate=pl.CostEstimate(
            flops=2 * pairs * depth * 16 * BLOCK, bytes_accessed=4 * pairs * depth, transcendentals=0
        ),
        name="ladder",
    )(amplitudes, integrals)
    return residual_in + ladder


def solution(mesh):
    placed = (P("row", "col"), P("row", "col"), P("col", "row"))
    return jax.shard_map(
        on_device, mesh=mesh, in_specs=placed, out_specs=P("col", "row"), check_vma=False
    )
```

profile of v0, /device:TPU:16, one launch (start us, length us, event | category | flops | bytes accessed | tf_op | source)
XLA Modules:
  0.0 158.2 jit_solution(6700636719485613772)
XLA Ops:
  0.0 0.0 copy-start
  0.0 157.5 %ladder.1 = f32[64,400]{1,0:T(8,128)S(1)} custom-call(bf16[400,12544]{1,0:T(8,128)(2,1)} %amp.1, bf16[64,12544]{1,0:T(8,128)(2,1)} %integ.1), custom_call_target="tpu_custom_call" | custom-call | flops 10276044800 | bytes 20070400 | tf_op jit(solution)/shard_map/ladder/pallas_call | solution.py:587
  157.5 0.0 copy-done
  157.5 0.7 add.3
Async XLA Ops:
  0.0 157.5 %copy-start = (f32[64,400]{1,0:T(8,128)S(1)}, f32[64,400]{1,0:T(8,128)}, u32[]{:S(2)}) copy-start(f32[64,400]{1,0:T(8,128)} %param.5) | copy-start | bytes 307204
where the time goes:
time: 161 us; the launch traced here: 158 us
  Pallas kernels  158 us (98%)
    pallas_call x1, Pallas kernels, on_device(): pl.pallas_call(kernel, out_shape=jax.ShapeDtypeStruct((BLOCK, pairs), f32...  158 us

commit v1 on v0

--- a/solution.py
+++ b/solution.py
@@ -338,7 +338,8 @@
         return remote(src.at[t], dst.at[row], send.at[t, h], recv.at[row], dev(hx_=h, y_=hx, z_=t))
 
     def each_mirror(act):
-        def body(t, _):
+        def body(step, _):
+            t = (z + RING // 2 + step) % RING
             for h in range(2):
 
                 @pl.when(jnp.logical_not(is_me(h, hx, t)))
@@ -385,7 +386,8 @@
         return remote(src, from_all.at[col // 2], all_s.at[q, h], all_r.at[col // 2], ((1 - y) * RING + z, owner))
 
     def each_owner(act):
-        def body(q, _):
+        def body(step, _):
+            q = (step + col // 4) % (RING // 2)
             for h in range(2):
                 act(to_owner(q, h))
             return 0

time: 161 us -> 161 us (level)
  no operation moved by 1% of the time
where the time goes in v1:
time: 161 us; the launch traced here: 159 us
  Pallas kernels  158 us (98%)
    pallas_call x1, Pallas kernels, on_device(): pl.pallas_call(kernel, out_shape=jax.ShapeDtypeStruct((BLOCK, pairs), f32...  158 us

profile of v1, /device:TPU:16, one launch (start us, length us, event | category | flops | bytes accessed | tf_op | source)
XLA Modules:
  0.0 158.6 jit_solution(6642460597639927378)
XLA Ops:
  0.0 0.0 copy-start
  0.0 157.9 %ladder.1 = f32[64,400]{1,0:T(8,128)S(1)} custom-call(bf16[400,12544]{1,0:T(8,128)(2,1)} %amp.1, bf16[64,12544]{1,0:T(8,128)(2,1)} %integ.1), custom_call_target="tpu_custom_call" | custom-call | flops 10276044800 | bytes 20070400 | tf_op jit(solution)/shard_map/ladder/pallas_call | solution.py:589
  157.9 0.0 copy-done
  157.9 0.7 add.3
Async XLA Ops:
  0.0 157.9 %copy-start = (f32[64,400]{1,0:T(8,128)S(1)}, f32[64,400]{1,0:T(8,128)}, u32[]{:S(2)}) copy-start(f32[64,400]{1,0:T(8,128)} %param.5) | copy-start | bytes 307204
